TPU v7x, 32 devices: a whole 2x2x4 slice. The times are simulated.
32 devices in a mesh: groups: 2 (over y), wide: 16 (over z, x, core).
Axes of the slice: x: 2, y: 2, z: 4, core: 2. Of those that a mesh axis runs over, the one named last changes fastest.
Arguments:
- prefill_state: bfloat16 [128, 128, 4096], P('groups', None, 'wide'), parts along dimension 0, may hold values from -6 to 6
- residual_in: bfloat16 [128, 4, 2048], P(('groups', 'wide')), parts along dimension 0, may hold values from -3 to 3
- queries: bfloat16 [128, 4, 2048], P(('groups', 'wide')), parts along dimension 0, may hold values from -6 to 6
- keys_in: bfloat16 [128, 4, 2048], P(('groups', 'wide')), parts along dimension 0, may hold values from -6 to 6
- values_in: bfloat16 [128, 4, 4096], P(('groups', 'wide')), parts along dimension 0, may hold values from -6 to 6
- gate_in: bfloat16 [128, 4, 4096], P(('groups', 'wide')), parts along dimension 0, may hold values from -6 to 6
- beta_rate: bfloat16 [128, 4, 32], P(('groups', 'wide')), parts along dimension 0, may hold values from 0.099609375 to 0.8984375
- decay_rate: bfloat16 [128, 4, 32], P(('groups', 'wide')), parts along dimension 0, may hold values from 0.3984375 to 1
- norm_gain: float32 [128], replicated, may hold values from 0.5 to 1.5
- out_weight: bfloat16 [4096, 2048], P('wide'), may hold values from -0.09375 to 0.09375
- post_gain: float32 [2048], replicated, may hold values from 0.5 to 1.5
- router_weight: bfloat16 [2048, 128], replicated, may hold values from -0.375 to 0.375
- expert_ids: int32 [128, 4, 10], P(('groups', 'wide')), parts along dimension 0, may hold values from 0 to 127, all different within a row; in each aligned block of 16 rows (0 to 15, 16 to 31, ..., all dimensions but the last counted through in order) at most 2 rows name the same one
- expert_gate: bfloat16 [128, 2048, 512], P('wide'), may hold values from -0.125 to 0.125
- expert_up: bfloat16 [128, 2048, 512], P('wide'), may hold values from -0.125 to 0.125
- expert_down: bfloat16 [128, 512, 2048], P('wide'), may hold values from -0.25 to 0.25
Outputs:
- mixed: bfloat16 [128, 4, 2048], P(('groups', 'wide')), parts along dimension 0
There are 2 independent parts, one for each index of `groups`. A program takes and returns all parts, laid end to end along the dimension named above; an argument that names none is the same for every part. Nothing has to cross between parts.
Inputs may be any that keep to these rules, and one draw needn't show every extreme that they name: `expert_ids`: each row names 10 different experts. In each aligned block of 16 rows (the requests of one device at all steps) no expert is named by more than 2 rows, and in every draw some expert is named by exactly 2 rows of a block.
All inputs are finite; a program needn't handle non-finite values.
Results may differ from a plain program's by a relative error of at most 0.0051.
Values may be sent and summed in bfloat16 or wider, within the bound.
A program may use at most 192 MiB of HBM per device.

v0:
```python
import jax
import jax.numpy as jnp
from jax import lax
from jax.sharding import PartitionSpec as P

TOPK = 10
CAP = 2


def unit_rows(vectors):
    vectors = vectors.astype(jnp.float32)
    return vectors * lax.rsqrt(jnp.sum(vectors * vectors, axis=-1, keepdims=True) + 1e-06)


def recurrence(carry_state, q_unit, k_unit, value_cols, beta_cols, decay_cols):
    results = []
    for step_idx in range(q_unit.shape[1]):
        carry_state = carry_state * decay_cols[:, step_idx][:, None]
        key_now = jnp.swapaxes(k_unit[:, step_idx], 1, 2)[..., None]
        predicted = jnp.einsum(
            "bdhc,bhd->bhc", carry_state, k_unit[:, step_idx], precision=lax.Precision.HIGHEST
        )
        change = beta_cols[:, step_idx] * (value_cols[:, step_idx] - predicted)
        carry_state = carry_state + key_now * change[:, None]
        results.append(
            jnp.einsum(
                "bdhc,bhd->bhc", carry_state, q_unit[:, step_idx], precision=lax.Precision.HIGHEST
            )
        )
    return jnp.stack(results, axis=1)


def local_heads(prefill_state, queries, keys_in, values_in, gate_in, beta_rate, decay_rate, norm_gain):
    owned_req, num_steps, _ = queries.shape
    total_req, key_dim, columns = prefill_state.shape
    head_dim = norm_gain.shape[0]
    wide_size = lax.axis_size("wide")
    group = columns // head_dim

    def by_head(array):
        return array.reshape(owned_req, num_steps, wide_size, -1)

    packed = jnp.concatenate(
        [by_head(a) for a in (queries, keys_in, values_in, gate_in, beta_rate, decay_rate)], axis=-1
    )
    got = lax.all_to_all(packed, "wide", split_axis=2, concat_axis=0, tiled=True)[:, :, 0]
    q_raw, k_raw, v_raw, g_raw, beta, decay = jnp.split(
        got,
        [key_dim, 2 * key_dim, 2 * key_dim + columns, 2 * key_dim + 2 * columns, 2 * key_dim + 2 * columns + group],
        axis=-1,
    )

    def inverse_norm(vectors):
        vectors = vectors.astype(jnp.float32)
        return lax.rsqrt(jnp.sum(vectors * vectors, axis=-1) + 1e-06)

    q_inv, k_inv = inverse_norm(q_raw), inverse_norm(k_raw)
    both = jnp.concatenate([k_raw, q_raw], axis=1)
    from_state = jnp.einsum("rsd,rdc->rsc", both, prefill_state, preferred_element_type=jnp.float32)
    gram = jnp.einsum("rsd,rtd->rst", both, k_raw, preferred_element_type=jnp.float32)
    gram = gram * jnp.concatenate([k_inv, q_inv], axis=1)[:, :, None] * k_inv[:, None, :]
    from_state = from_state * jnp.concatenate([k_inv, q_inv], axis=1)[:, :, None]

    def widen(rates):
        return jnp.repeat(rates.astype(jnp.float32), head_dim, axis=-1)

    beta, decay = widen(beta), widen(decay)
    value_cols = v_raw.astype(jnp.float32)
    through = jnp.ones_like(decay[:, 0])
    changes, results = [], []
    for t in range(num_steps):
        through = through * decay[:, t]
        changes = [c * decay[:, t] for c in changes]
        predicted = through * from_state[:, t]
        attended = through * from_state[:, num_steps + t]
        for s, c in enumerate(changes):
            predicted = predicted + gram[:, t, s][:, None] * c
            attended = attended + gram[:, num_steps + t, s][:, None] * c
        now = beta[:, t] * (value_cols[:, t] - predicted)
        attended = attended + gram[:, num_steps + t, t][:, None] * now
        changes.append(now)
        results.append(attended)
    heads_view = jnp.stack(results, axis=1).reshape(total_req * num_steps, group, head_dim)
    scale = lax.rsqrt(jnp.mean(heads_view * heads_view, axis=-1, keepdims=True) + 1e-06)
    gate_act = jax.nn.silu(g_raw.astype(jnp.float32)).reshape(heads_view.shape)
    normed = (heads_view * scale * norm_gain * gate_act).astype(jnp.bfloat16)
    return normed.reshape(total_req * num_steps, columns)


def moved_heads(prefill_state, queries, keys_in, values_in, gate_in, beta_rate, decay_rate, norm_gain):
    wide_size = lax.axis_size("wide")
    owned_req = queries.shape[0]
    num_steps = queries.shape[1]
    local_rows = owned_req * num_steps
    key_dim = prefill_state.shape[1]
    columns = prefill_state.shape[2]
    head_dim = norm_gain.shape[0]
    hv_dv = values_in.shape[2]
    value_heads = hv_dv // head_dim
    key_heads = queries.shape[2] // key_dim
    key_group = hv_dv // key_heads
    arrived = lax.all_to_all(prefill_state, "wide", split_axis=0, concat_axis=2, tiled=True)
    carry_state = arrived.astype(jnp.float32).reshape(owned_req, key_dim, key_heads, key_group)
    q_unit = unit_rows(queries.reshape(owned_req, num_steps, key_heads, key_dim))
    k_unit = unit_rows(keys_in.reshape(owned_req, num_steps, key_heads, key_dim))
    value_cols = values_in.astype(jnp.float32).reshape(owned_req, num_steps, key_heads, key_group)
    beta_cols = jnp.repeat(beta_rate.astype(jnp.float32), head_dim, axis=-1).reshape(
        owned_req, num_steps, key_heads, key_group
    )
    decay_cols = jnp.repeat(decay_rate.astype(jnp.float32), head_dim, axis=-1).reshape(
        owned_req, num_steps, key_heads, key_group
    )
    attended = recurrence(carry_state, q_unit, k_unit, value_cols, beta_cols, decay_cols).reshape(
        local_rows, hv_dv
    )
    heads_view = attended.reshape(local_rows, value_heads, head_dim)
    scale = lax.rsqrt(jnp.mean(heads_view * heads_view, axis=-1, keepdims=True) + 1e-06)
    gate_act = jax.nn.silu(gate_in.reshape(local_rows, value_heads, head_dim).astype(jnp.float32))
    normed = (
        (heads_view * scale * norm_gain * gate_act).astype(jnp.bfloat16).reshape(local_rows, hv_dv)
    )
    return lax.all_to_all(
        normed.reshape(local_rows, wide_size, columns),
        "wide",
        split_axis=1,
        concat_axis=0,
        tiled=True,
    ).reshape(wide_size * local_rows, columns)


def per_device(
    prefill_state,
    residual_in,
    queries,
    keys_in,
    values_in,
    gate_in,
    beta_rate,
    decay_rate,
    norm_gain,
    out_weight,
    post_gain,
    router_weight,
    expert_ids,
    expert_gate,
    expert_up,
    expert_down,
):
    wide_size = lax.axis_size("wide")
    owned_req = queries.shape[0]
    num_steps = queries.shape[1]
    local_rows = owned_req * num_steps
    key_dim = prefill_state.shape[1]
    columns = prefill_state.shape[2]
    head_dim = norm_gain.shape[0]
    hv_dv = values_in.shape[2]
    value_heads = hv_dv // head_dim
    key_heads = queries.shape[2] // key_dim
    key_group = hv_dv // key_heads
    width = residual_in.shape[2]
    heads = local_heads if key_heads == wide_size else moved_heads
    spread = heads(
        prefill_state, queries, keys_in, values_in, gate_in, beta_rate, decay_rate, norm_gain
    )
    attention = lax.psum_scatter(
        jnp.dot(spread, out_weight, preferred_element_type=jnp.float32),
        "wide",
        scatter_dimension=0,
        tiled=True,
    )
    hidden = residual_in.reshape(local_rows, width).astype(jnp.float32) + attention
    moe_in = (
        hidden * lax.rsqrt(jnp.mean(hidden * hidden, axis=-1, keepdims=True) + 1e-06) * post_gain
    ).astype(jnp.bfloat16)
    logits = jnp.dot(moe_in, router_weight, preferred_element_type=jnp.float32)
    num_experts = router_weight.shape[1]
    flat_ids = expert_ids.reshape(local_rows, TOPK)
    onehot = flat_ids[:, :, None] == jnp.arange(num_experts, dtype=jnp.int32)[None, None, :]
    chosen = jnp.sum(jnp.where(onehot, logits[:, None, :], 0.0), axis=-1)
    squashed = jax.nn.sigmoid(chosen)
    gates = squashed / jnp.sum(squashed, axis=1, keepdims=True)
    counts_flat = onehot.reshape(local_rows * TOPK, num_experts).astype(jnp.int32)
    running = jnp.cumsum(counts_flat, axis=0) - 1
    slot_of = jnp.sum(counts_flat * running, axis=1).reshape(local_rows, TOPK)
    position = flat_ids * CAP + slot_of
    dispatch = jnp.any(
        position[:, :, None] == jnp.arange(num_experts * CAP, dtype=jnp.int32)[None, None, :],
        axis=1,
    ).astype(jnp.bfloat16)
    buffer = jnp.einsum("rs,rd->sd", dispatch, moe_in, preferred_element_type=jnp.float32).astype(
        jnp.bfloat16
    )
    exp_dev = expert_gate.shape[0]
    buffer = buffer.reshape(wide_size, exp_dev, CAP, width)
    slab_in = lax.all_to_all(buffer, "wide", split_axis=0, concat_axis=0, tiled=True)
    gate_part = jnp.einsum(
        "sekd,edf->sekf", slab_in, expert_gate, preferred_element_type=jnp.float32
    )
    up_part = jnp.einsum("sekd,edf->sekf", slab_in, expert_up, preferred_element_type=jnp.float32)
    hidden_mid = (jax.nn.silu(gate_part) * up_part).astype(jnp.bfloat16)
    processed = jnp.einsum(
        "sekf,efd->sekd", hidden_mid, expert_down, preferred_element_type=jnp.float32
    ).astype(jnp.bfloat16)
    returned = lax.all_to_all(processed, "wide", split_axis=0, concat_axis=0, tiled=True).reshape(
        num_experts * CAP, width
    )
    picked = returned[position]
    combined = jnp.sum(gates[:, :, None] * picked.astype(jnp.float32), axis=1)
    return (hidden + combined).astype(jnp.bfloat16).reshape(owned_req, num_steps, width)


def solution(mesh):
    return jax.shard_map(
        per_device,
        mesh=mesh,
        in_specs=(
            P("groups", None, "wide"),
            P(("groups", "wide"), None, None),
            P(("groups", "wide"), None, None),
            P(("groups", "wide"), None, None),
            P(("groups", "wide"), None, None),
            P(("groups", "wide"), None, None),
            P(("groups", "wide"), None, None),
            P(("groups", "wide"), None, None),
            P(),
            P("wide", None),
            P(),
            P(),
            P(("groups", "wide"), None, None),
            P("wide", None, None),
            P("wide", None, None),
            P("wide", None, None),
        ),
        out_specs=P(("groups", "wide"), None, None),
        check_vma=False,
    )
```

profile of v0, /device:TPU:0, one launch (start us, length us, event | category | flops | bytes accessed | tf_op | source)
XLA Modules:
  0.0 202.8 jit_solution(2221632431951229678)
XLA Ops:
  6.5 1.1 reshape.311
  7.6 1.0 reshape.312
  8.6 0.8 copy.161
  9.4 0.5 copy.163
  9.9 0.8 copy.162
  10.7 0.5 copy.164
  11.3 0.9 reshape.309
  12.2 0.9 reshape.310
  13.2 1.1 copy.165
  14.3 7.4 %all-to-all-start = ((bf16[4,4,16,772]{3,0,1,2:T(4,128)(2,1)}), bf16[4,4,16,772]{3,0,1,2:T(4,128)(2,1)S(1)}, u32[]{:S(2)}, u32[]{:S(2)}) async-start(bf16[4,4,16,772]{3,0,1,2:T(4,128)(2,1)} %copy.165), calls=%async_computation | async-start | bytes 917504 | tf_op jit(solution)/shard_map/all_to_all | solution.py:46
  21.7 0.7 broadcast_bitcast_fusion
  22.4 12.5 %all-to-all-done = bf16[4,4,16,772]{3,0,1,2:T(4,128)(2,1)S(1)} async-done(((bf16[4,4,16,772]{3,0,1,2:T(4,128)(2,1)}), bf16[4,4,16,772]{3,0,1,2:T(4,128)(2,1)S(1)}, u32[]{:S(2)}, u32[]{:S(2)}) %all-to-all-start) | async-done | bytes 395296 | tf_op jit(solution)/shard_map/all_to_all | solution.py:46
  36.3 4.0 %slice_reduce_fusion.15 = (f32[64]{0:T(128)S(1)}, f32[64]{0:T(128)S(1)}, f32[64]{0:T(128)S(1)}, f32[64]{0:T(128)S(1)}, f32[64]{0:T(128)S(1)}, /*index=5*/f32[64]...) fusion(f32[64,8,4]{1,2,0:T(4,128)S(1)} %fusion.24), kind=kLoop, calls=%fused_computation.112 | loop fusion | bytes 8192 | tf_op jit(solution)/shard_map/slice | solution.py:80
  40.3 2.8 %fusion.40 = f32[64,8,256]{2,1,0:T(8,128)S(1)} fusion(bf16[64,128,256]{2,1,0:T(8,128)(2,1)} %param.16, bf16[64,8,128]{2,0,1:T(8,128)(2,1)S(1)} %pad_maximum_fusion.1), kind=kOutput, calls=%fused_computation.46 | convolution fusion | flops 33554432 | bytes 4849664 | tf_op jit(solution)/shard_map/rsd,rdc->rsc/dot_general | solution.py:59
  45.4 0.3 reduce_sum.74
  46.7 1.8 fusion.34
  49.4 60.0 %reduce-scatter.2.cloned.1.call-done = f32[16,2048]{1,0:T(8,128)} async-done(((f32[256,2048]{1,0:T(8,128)}), f32[16,2048]{1,0:T(8,128)}) %reduce-scatter.2.cloned.1.call-update) | async-done | bytes 131088 | tf_op jit(solution)/shard_map/reduce_scatter | solution.py:165
  109.4 1.0 multiply_reduce_fusion.1
  110.5 0.5 convolution_convert_fusion
  111.0 0.7 reshape.322
  111.7 28.4 %all_to_all.25 = bf16[16,8,2,2048]{3,2,1,0:T(2,128)(2,1)S(1)} all-to-all(bf16[16,8,2,2048]{3,2,1,0:T(2,128)(2,1)S(1)} %reshape.322), channel_id=1, replica_groups=mesh['groups'=2,'wide'=16] {'wide'}, dimensions={0} | all-to-all | bytes 2097152 | tf_op jit(solution)/shard_map/all_to_all | solution.py:195
  140.0 9.0 %fusion.12 = f32[16,8,2,512]{3,0,2,1:T(8,128)S(1)} fusion(bf16[8,2048,512]{2,1,0:T(8,128)(2,1)} %param.29, bf16[16,8,2,2048]{3,2,1,0:T(2,128)(2,1)S(1)} %all_to_all.25), kind=kOutput, calls=%fused_computation.11 | convolution fusion | flops 536870912 | bytes 18350080 | tf_op jit(solution)/shard_map/sekd,edf->sekf/dot_general | solution.py:196
  149.1 9.1 %fusion.21 = bf16[16,8,2,512]{3,0,2,1:T(8,128)(2,1)S(1)} fusion(bf16[8,2048,512]{2,1,0:T(8,128)(2,1)} %param.30, bf16[16,8,2,2048]{3,2,1,0:T(2,128)(2,1)S(1)} %all_to_all.25, f32[16,8,2,512]{3,0,2,1:T(8,128)S(1)} %fusion.12), kind=kOutput, calls=%fused_computation.14 | convolution fusion | flops 537657344 | bytes 18612224 | tf_op jit(solution)/shard_map/sekd,edf->sekf/dot_general | solution.py:199
  158.2 3.0 %fusion.9 = bf16[16,8,2,2048]{3,0,2,1:T(8,128)(2,1)S(1)} fusion(bf16[16,8,2,512]{3,0,2,1:T(8,128)(2,1)S(1)} %fusion.21, bf16[8,512,2048]{2,1,0:T(8,128)(2,1)S(1)} %bitcast.79), kind=kOutput, calls=%fused_computation.9 | convolution fusion | flops 537395200 | bytes 18087936 | tf_op jit(solution)/shard_map/sekf,efd->sekd/dot_general | solution.py:201
  161.2 2.1 %copy.186 = bf16[16,8,2,2048]{3,2,1,0:T(2,128)(2,1)} copy(bf16[16,8,2,2048]{3,0,2,1:T(8,128)(2,1)S(1)} %fusion.9) | data formatting | bytes 2097152 | tf_op jit(solution)/shard_map/convert_element_type | solution.py:203
  163.3 5.0 %all-to-all-start.2 = ((bf16[16,8,2,2048]{3,2,1,0:T(2,128)(2,1)}), bf16[16,8,2,2048]{3,2,1,0:T(2,128)(2,1)S(1)}, u32[]{:S(2)}, u32[]{:S(2)}) async-start(bf16[16,8,2,2048]{3,2,1,0:T(2,128)(2,1)} %copy.186), calls=%async_computation.3 | async-start | bytes 2097152 | tf_op jit(solution)/shard_map/all_to_all | solution.py:204
  169.1 22.1 %all-to-all-done.2 = bf16[16,8,2,2048]{3,2,1,0:T(2,128)(2,1)S(1)} async-done(((bf16[16,8,2,2048]{3,2,1,0:T(2,128)(2,1)}), bf16[16,8,2,2048]{3,2,1,0:T(2,128)(2,1)S(1)}, u32[]{:S(2)}, u32[]{:S(2)}) %all-to-all-start.2) | async-done | bytes 1048608 | tf_op jit(solution)/shard_map/all_to_all | solution.py:204
  191.2 0.4 reshape.323
  191.7 1.9 gather_fusion
  193.5 1.2 reshape.337
  194.8 0.5 multiply_reduce_fusion
  195.3 0.7 reshape.325
  (85 shorter events, 6.3 us)
Async XLA Ops:
  6.5 40.1 %copy-start = (bf16[256,2048]{1,0:T(8,128)(2,1)S(1)}, bf16[256,2048]{1,0:T(8,128)(2,1)}, u32[]{:S(2)}) copy-start(bf16[256,2048]{1,0:T(8,128)(2,1)} %param.25) | copy-start | bytes 3145732
  6.5 41.9 %copy-start.4 = (bf16[4,4,2048]{2,1,0:T(4,128)(2,1)S(1)}, bf16[4,4,2048]{2,1,0:T(4,128)(2,1)}, u32[]{:S(2)}) copy-start(bf16[4,4,2048]{2,1,0:T(4,128)(2,1)} %param.17) | copy-start | bytes 196612
  6.5 42.0 %copy-start.3 = (s32[4,4,10]{2,1,0:T(4,128)S(1)}, s32[4,4,10]{2,1,0:T(4,128)}, u32[]{:S(2)}) copy-start(s32[4,4,10]{2,1,0:T(4,128)} %param.28) | copy-start | bytes 1924
  6.5 103.9 %copy-start.5 = (f32[2048]{0:T(1024)S(1)}, f32[2048]{0:T(1024)}, u32[]{:S(2)}) copy-start(f32[2048]{0:T(1024)} %param.26) | copy-start | bytes 24580
  14.3 20.6 %all-to-all-start = ((bf16[4,4,16,772]{3,0,1,2:T(4,128)(2,1)}), bf16[4,4,16,772]{3,0,1,2:T(4,128)(2,1)S(1)}, u32[]{:S(2)}, u32[]{:S(2)}) async-start(bf16[4,4,16,772]{3,0,1,2:T(4,128)(2,1)} %copy.165), calls=%async_computation | async-start | bytes 917504 | tf_op jit(solution)/shard_map/all_to_all | solution.py:46
  21.7 87.7 %reduce-scatter.2.cloned.1.call-start = ((), (), s32[]{:S(2)}) async-start(), calls=%async_computation.4 | async-start | bytes 2228224 | tf_op jit(solution)/shard_map/reduce_scatter | solution.py:165
  140.0 18.1 %slice-start = ((s8[16777216]{0:T(1024)(128)(4,1)}), s8[4194304]{0:T(1024)(128)(4,1)S(1)}, s32[]{:S(2)}) async-start(s8[16777216]{0:T(1024)(128)(4,1)} %bitcast.78), calls=%async_computation.5 | async-start | bytes 8388608
  140.0 18.1 %slice-start.1 = ((s8[16777216]{0:T(1024)(128)(4,1)}), s8[4194304]{0:T(1024)(128)(4,1)S(1)}, s32[]{:S(2)}) async-start(s8[16777216]{0:T(1024)(128)(4,1)} %bitcast.78), calls=%async_computation.6 | async-start | bytes 8388608
  149.1 9.1 %slice-start.2 = ((s8[16777216]{0:T(1024)(128)(4,1)}), s8[4194304]{0:T(1024)(128)(4,1)S(1)}, s32[]{:S(2)}) async-start(s8[16777216]{0:T(1024)(128)(4,1)} %bitcast.78), calls=%async_computation.7 | async-start | bytes 8388608
  149.1 9.2 %slice-start.3 = ((s8[16777216]{0:T(1024)(128)(4,1)}), s8[4194304]{0:T(1024)(128)(4,1)S(1)}, s32[]{:S(2)}) async-start(s8[16777216]{0:T(1024)(128)(4,1)} %bitcast.78), calls=%async_computation.8 | async-start | bytes 8388608
  149.1 19.5 %copy-start.2 = (bf16[2048,128]{1,0:T(8,128)(2,1)S(1)}, bf16[2048,128]{1,0:T(8,128)(2,1)}, u32[]{:S(2)}) copy-start(bf16[2048,128]{1,0:T(8,128)(2,1)} %param.27) | copy-start | bytes 1572868
  149.1 46.8 %copy-start.1 = (bf16[256,2048]{1,0:T(8,128)(2,1)S(1)}, bf16[256,2048]{1,0:T(8,128)(2,1)}, u32[]{:S(2)}) copy-start(bf16[256,2048]{1,0:T(8,128)(2,1)} %param.25) | copy-start | bytes 3145732
  163.3 27.9 %all-to-all-start.2 = ((bf16[16,8,2,2048]{3,2,1,0:T(2,128)(2,1)}), bf16[16,8,2,2048]{3,2,1,0:T(2,128)(2,1)S(1)}, u32[]{:S(2)}, u32[]{:S(2)}) async-start(bf16[16,8,2,2048]{3,2,1,0:T(2,128)(2,1)} %copy.186), calls=%async_computation.3 | async-start | bytes 2097152 | tf_op jit(solution)/shard_map/all_to_all | solution.py:204
Sparse Core Ops, SparseCore 0:
  48.6 60.7 reduce-scatter.1
where the time goes:
time: 205 us; the launch traced here: 203 us
  waiting for transfers between devices  94.6 us (46%)
  blocking collectives  28.4 us (14%)
  matrix products  26.7 us (13%)
  local copies, waits for them, and re-layouts  23 us (11%)
  between operations  13.9 us (7%)
  starting transfers between devices  12.4 us (6%)
  other arithmetic  3.84 us (2%)
    reduce_scatter x1, waiting for transfers between devices, per_device(): lax.psum_scatter(jnp.dot(spread, out_weight, preferred_element_type=jnp.f...  60 us
    all_to_all x1, blocking collectives, per_device(): lax.all_to_all(buffer, 'wide', split_axis=0, concat_axis=0, tiled=True)  28.4 us
    all_to_all x1, waiting for transfers between devices, per_device(): lax.all_to_all(processed, 'wide', split_axis=0, concat_axis=0, tiled=True)  22.1 us
    all_to_all x1, waiting for transfers between devices, local_heads(): lax.all_to_all(packed, 'wide', split_axis=2, concat_axis=0, tiled=True)  12.5 us
    dot_general x1, matrix products, per_device(): jnp.einsum('sekd,edf->sekf', slab_in, expert_up, preferred_element_type=j...  9.08 us
    dot_general x1, matrix products, per_device(): jnp.einsum('sekd,edf->sekf', slab_in, expert_gate, preferred_element_type...  9.01 us
    all_to_all x1, starting transfers between devices, local_heads(): lax.all_to_all(packed, 'wide', split_axis=2, concat_axis=0, tiled=True)  7.36 us
    all_to_all x1, starting transfers between devices, per_device(): lax.all_to_all(processed, 'wide', split_axis=0, concat_axis=0, tiled=True)  4.99 us
  transfers between devices with their start and end apart: 3, of which 3 were waited for; matrix products, arithmetic and copies ran while one was open for 1% of the time, Pallas kernels for 0%

commit v1 on v0

--- a/solution.py
+++ b/solution.py
@@ -1,6 +1,10 @@
+import functools
+
 import jax
 import jax.numpy as jnp
 from jax import lax
+from jax.experimental import pallas as pl
+from jax.experimental.pallas import tpu as pltpu
 from jax.sharding import PartitionSpec as P
 
 TOPK = 10
@@ -126,6 +130,317 @@
         concat_axis=0,
         tiled=True,
     ).reshape(wide_size * local_rows, columns)
+
+
+def dot(left, right):
+    return jnp.dot(left, right, preferred_element_type=jnp.float32)
+
+
+def dot_nt(left, right):
+    return lax.dot_general(
+        left, right, (((1,), (1,)), ((), ())), preferred_element_type=jnp.float32
+    )
+
+
+def layer_kernel(
+    sizes,
+    heads_ref,
+    out_w_ref,
+    resid_ref,
+    post_ref,
+    router_ref,
+    ids_ref,
+    gate_hbm,
+    up_hbm,
+    down_hbm,
+    mixed_ref,
+    gate_w,
+    up_w,
+    down_w,
+    core_send,
+    core_recv,
+    x_send,
+    x_recv,
+    z_send,
+    z_recv,
+    part,
+    lane_part,
+    hidden,
+    tokens,
+    slab,
+    outcome,
+    pick_hi,
+    pick_lo,
+    w_sem,
+    rs_send_sem,
+    rs_recv_sem,
+    ag_send_sem,
+    ag_recv_sem,
+):
+    wide_size, owned, width, experts, local_experts, held = sizes
+    num_z = wide_size // 4
+    rows = wide_size * owned
+    half = rows // 2
+    me = lax.axis_index("wide")
+    core = lax.rem(me, 2)
+    x = lax.rem(me // 2, 2)
+    z = me // 4
+
+    def device_at(at_z, at_x, at_core):
+        return at_z * 4 + at_x * 2 + at_core
+
+    def z_ahead(d):
+        return lax.rem(z + d, num_z)
+
+    def z_behind(d):
+        return lax.rem(z + num_z - d, num_z)
+
+    core_mate = device_at(z, x, 1 - core)
+    x_mate = device_at(z, 1 - x, core)
+    z_mates = [device_at(z_ahead(d), x, core) for d in range(1, num_z)]
+
+    def weight_copies(e, slot):
+        return [
+            pltpu.make_async_copy(hbm.at[e], vmem.at[slot], w_sem.at[i, slot])
+            for i, (hbm, vmem) in enumerate(((gate_hbm, gate_w), (up_hbm, up_w), (down_hbm, down_w)))
+        ]
+
+    for e in range(held):
+        for copy in weight_copies(e, e):
+            copy.start()
+
+    barrier = pltpu.get_barrier_semaphore()
+    for mate in [core_mate, x_mate] + z_mates:
+        pl.semaphore_signal(
+            barrier, inc=1, device_id={"wide": mate}, device_id_type=pl.DeviceIdType.MESH
+        )
+    pl.semaphore_wait(barrier, 1 + num_z)
+
+    def remote(src, dst, send_sem, recv_sem, mate):
+        return pltpu.make_async_remote_copy(
+            src_ref=src,
+            dst_ref=dst,
+            send_sem=send_sem,
+            recv_sem=recv_sem,
+            device_id={"wide": mate},
+            device_id_type=pl.DeviceIdType.MESH,
+        )
+
+    def reduce_scatter(turn, produce):
+        def exchange(i, src, dst, mate):
+            copy = remote(src, dst, rs_send_sem.at[turn, i], rs_recv_sem.at[turn, i], mate)
+            copy.start()
+            return copy
+
+        core_send[turn] = produce(1 - core).astype(jnp.bfloat16).reshape(num_z, 2, owned, width)
+        to_core = exchange(0, core_send.at[turn], core_recv.at[turn], core_mate)
+        part[...] = produce(core).reshape(num_z, 2, owned, width)
+        to_core.wait()
+        x_send[turn] = (part[:, 1 - x] + core_recv[turn, :, 1 - x].astype(jnp.float32)).astype(
+            jnp.bfloat16
+        )
+        to_x = exchange(1, x_send.at[turn], x_recv.at[turn], x_mate)
+        lane_part[...] = part[:, x] + core_recv[turn, :, x].astype(jnp.float32)
+        to_x.wait()
+        to_z = []
+        for d in range(1, num_z):
+            at_z = z_ahead(d)
+            z_send[turn, d - 1] = (
+                lane_part[at_z] + x_recv[turn, at_z].astype(jnp.float32)
+            ).astype(jnp.bfloat16)
+            to_z.append(
+                exchange(1 + d, z_send.at[turn, d - 1], z_recv.at[turn, d - 1], z_mates[d - 1])
+            )
+        total = lane_part[z] + x_recv[turn, z].astype(jnp.float32)
+        for d in range(1, num_z):
+            to_z[d - 1].wait()
+            total = total + z_recv[turn, d - 1].astype(jnp.float32)
+        return total
+
+    def project(at_core):
+        return dot(heads_ref[:, at_core].reshape(half, heads_ref.shape[-1]), out_w_ref[...])
+
+    now = resid_ref[...].astype(jnp.float32) + reduce_scatter(0, project)
+    hidden[...] = now
+    moe_in = now * lax.rsqrt(jnp.mean(now * now, axis=-1, keepdims=True) + 1e-06) * post_ref[...]
+    tokens[me, :, :width] = moe_in.astype(jnp.bfloat16)
+    tokens[me, :, width:] = ids_ref[...]
+
+    sent = []
+
+    def pass_on(block, mate):
+        copy = remote(
+            tokens.at[block],
+            tokens.at[block],
+            ag_send_sem.at[len(sent)],
+            ag_recv_sem.at[block],
+            mate,
+        )
+        copy.start()
+        sent.append(copy)
+
+    def arrived(block, mate):
+        remote(
+            tokens.at[block], tokens.at[block], ag_send_sem.at[0], ag_recv_sem.at[block], mate
+        ).wait_recv()
+
+    for mate in z_mates:
+        pass_on(me, mate)
+    pass_on(me, x_mate)
+    pass_on(me, core_mate)
+    arrived(x_mate, x_mate)
+    pass_on(x_mate, core_mate)
+    for d in range(1, num_z):
+        block = device_at(z_behind(d), x, core)
+        arrived(block, x_mate)
+        pass_on(block, x_mate)
+        pass_on(block, core_mate)
+    for d in range(1, num_z):
+        block = device_at(z_behind(d), 1 - x, core)
+        arrived(block, x_mate)
+        pass_on(block, core_mate)
+    for at_z in range(num_z):
+        for at_x in range(2):
+            arrived(device_at(at_z, at_x, 1 - core), core_mate)
+    for copy in sent:
+        copy.wait_send()
+
+    everyone = tokens[...].reshape(rows, width + 128)
+    all_in = everyone[:, :width]
+    named = everyone[:, width:].astype(jnp.float32)
+    logits = dot(all_in, router_ref[...])
+    lanes = lax.broadcasted_iota(jnp.int32, (rows, experts), 1).astype(jnp.float32)
+    squashed = jnp.zeros((rows, experts), jnp.float32)
+    chosen = jnp.zeros((rows, experts), jnp.float32)
+    for k in range(TOPK):
+        chosen = jnp.where(named[:, k : k + 1] == lanes, 1.0, chosen)
+    squashed = jnp.where(chosen > 0.5, jax.nn.sigmoid(logits), 0.0)
+    gates = squashed / jnp.sum(squashed, axis=1, keepdims=True)
+    gates_hi = gates.astype(jnp.bfloat16)
+    gates_lo = (gates - gates_hi.astype(jnp.float32)).astype(jnp.bfloat16)
+    mine = (
+        lax.broadcasted_iota(jnp.int32, (local_experts, experts), 1)
+        == lax.broadcasted_iota(jnp.int32, (local_experts, experts), 0) + me * local_experts
+    )
+    mine = jnp.where(mine, 1.0, 0.0).astype(jnp.bfloat16)
+    hits = dot_nt(mine, chosen.astype(jnp.bfloat16))
+    local_hi = dot_nt(mine, gates_hi)
+    local_lo = dot_nt(mine, gates_lo)
+    row_a = lax.broadcasted_iota(jnp.int32, (rows, rows), 0)
+    row_b = lax.broadcasted_iota(jnp.int32, (rows, rows), 1)
+    earlier = (row_a // owned == row_b // owned) & (row_a < row_b)
+    rank = dot(hits.astype(jnp.bfloat16), jnp.where(earlier, 1.0, 0.0).astype(jnp.bfloat16))
+    origin = lax.broadcasted_iota(jnp.int32, (local_experts, rows), 1) // owned
+    place = jnp.where(hits > 0.5, (origin * CAP).astype(jnp.float32) + rank, -1.0)
+    slots = CAP * wide_size
+    slot_no = lax.broadcasted_iota(jnp.int32, (slots, rows), 0).astype(jnp.float32)
+    takes, takes_hi, takes_lo = [], [], []
+    for e in range(local_experts):
+        taken = place[e : e + 1] == slot_no
+        takes.append(jnp.where(taken, 1.0, 0.0))
+        takes_hi.append(jnp.where(taken, local_hi[e : e + 1], 0.0))
+        takes_lo.append(jnp.where(taken, local_lo[e : e + 1], 0.0))
+    take = jnp.concatenate(takes, axis=0).astype(jnp.bfloat16)
+    slab[...] = dot(take, all_in).astype(jnp.bfloat16).reshape(local_experts, slots, width)
+
+    def back(pieces):
+        turned = jnp.concatenate(pieces, axis=0).T.astype(jnp.bfloat16)
+        return turned.reshape(num_z * 2, 2, owned, local_experts * slots)
+
+    pick_hi[...] = back(takes_hi)
+    pick_lo[...] = back(takes_lo)
+
+    @pl.loop(0, local_experts)
+    def _(e):
+        slot = lax.rem(e, held)
+        for copy in weight_copies(e, slot):
+            copy.wait()
+        came = slab[e]
+        gate_part = dot(came, gate_w[slot])
+        up_part = dot(came, up_w[slot])
+        mid = (jax.nn.silu(gate_part) * up_part).astype(jnp.bfloat16)
+        outcome[e] = dot(mid, down_w[slot]).astype(jnp.bfloat16)
+
+        @pl.when(e + held < local_experts)
+        def _():
+            for copy in weight_copies(e + held, slot):
+                copy.start()
+
+    def combine(at_core):
+        results = outcome[...].reshape(local_experts * slots, width)
+        hi = pick_hi[:, at_core].reshape(half, local_experts * slots)
+        lo = pick_lo[:, at_core].reshape(half, local_experts * slots)
+        return dot(hi, results) + dot(lo, results)
+
+    mixed_ref[...] = (reduce_scatter(1, combine) + hidden[...]).astype(mixed_ref.dtype)
+
+
+def fused_layer(
+    spread, residual_in, out_weight, post_gain, router_weight, expert_ids, expert_gate, expert_up, expert_down
+):
+    wide_size = lax.axis_size("wide")
+    owned_req, num_steps, width = residual_in.shape
+    owned = owned_req * num_steps
+    rows = wide_size * owned
+    columns = spread.shape[1]
+    num_z = wide_size // 4
+    experts = router_weight.shape[1]
+    local_experts, _, hidden_units = expert_gate.shape
+    held = min(local_experts, 6)
+    slots = CAP * wide_size
+    ids = jnp.pad(
+        expert_ids.reshape(owned, TOPK), ((0, 0), (0, 128 - TOPK)), constant_values=-1
+    ).astype(jnp.bfloat16)
+    half16 = (2, num_z, 2, owned, width)
+    bf16, f32 = jnp.bfloat16, jnp.float32
+    vmem = pl.BlockSpec(memory_space=pltpu.VMEM)
+    hbm = pl.BlockSpec(memory_space=pl.ANY)
+    out = pl.pallas_call(
+        functools.partial(
+            layer_kernel, (wide_size, owned, width, experts, local_experts, held)
+        ),
+        out_shape=jax.ShapeDtypeStruct((owned, width), bf16),
+        in_specs=[vmem] * 6 + [hbm] * 3,
+        out_specs=vmem,
+        scratch_shapes=[
+            pltpu.VMEM((held, width, hidden_units), bf16),
+            pltpu.VMEM((held, width, hidden_units), bf16),
+            pltpu.VMEM((held, hidden_units, width), bf16),
+            pltpu.VMEM(half16, bf16),
+            pltpu.VMEM(half16, bf16),
+            pltpu.VMEM((2, num_z, owned, width), bf16),
+            pltpu.VMEM((2, num_z, owned, width), bf16),
+            pltpu.VMEM((2, num_z - 1, owned, width), bf16),
+            pltpu.VMEM((2, num_z - 1, owned, width), bf16),
+            pltpu.VMEM((num_z, 2, owned, width), f32),
+            pltpu.VMEM((num_z, owned, width), f32),
+            pltpu.VMEM((owned, width), f32),
+            pltpu.VMEM((wide_size, owned, width + 128), bf16),
+            pltpu.VMEM((local_experts, slots, width), bf16),
+            pltpu.VMEM((local_experts, slots, width), bf16),
+            pltpu.VMEM((num_z * 2, 2, owned, local_experts * slots), bf16),
+            pltpu.VMEM((num_z * 2, 2, owned, local_experts * slots), bf16),
+            pltpu.SemaphoreType.DMA((3, held)),
+            pltpu.SemaphoreType.DMA((2, 1 + num_z)),
+            pltpu.SemaphoreType.DMA((2, 1 + num_z)),
+            pltpu.SemaphoreType.DMA((wide_size,)),
+            pltpu.SemaphoreType.DMA((wide_size,)),
+        ],
+        compiler_params=pltpu.CompilerParams(
+            collective_id=0, has_side_effects=True, vmem_limit_bytes=60 * 1024 * 1024
+        ),
+    )(
+        spread.reshape(num_z * 2, 2, owned, columns),
+        out_weight,
+        residual_in.reshape(owned, width),
+        post_gain.reshape(1, width),
+        router_weight,
+        ids,
+        expert_gate,
+        expert_up,
+        expert_down,
+    )
+    return out.reshape(owned_req, num_steps, width)
 
 
 def per_device(
@@ -162,6 +477,18 @@
     spread = heads(
         prefill_state, queries, keys_in, values_in, gate_in, beta_rate, decay_rate, norm_gain
     )
+    if key_heads == wide_size == 16 and local_rows == 16 and router_weight.shape[1] == 128:
+        return fused_layer(
+            spread,
+            residual_in,
+            out_weight,
+            post_gain,
+            router_weight,
+            expert_ids,
+            expert_gate,
+            expert_up,
+            expert_down,
+        )
     attention = lax.psum_scatter(
         jnp.dot(spread, out_weight, preferred_element_type=jnp.float32),
         "wide",

time: 205 us -> 106 us (0.52)
  waiting for transfers between devices: 94.6 us -> 10.5 us
  Pallas kernels: 0 us -> 62.6 us
  blocking collectives: 28.4 us -> 0 us
  matrix products: 26.7 us -> 3.08 us
  between operations: 13.9 us -> 0.25 us
  starting transfers between devices: 12.4 us -> 7.36 us
  local copies, waits for them, and re-layouts: 23 us -> 18.4 us
    pallas_call x0 -> x1, Pallas kernels: none -> 62.6 us  [fused_layer(): pl.pallas_call(functools.partial(layer_kernel, (wide_size, owned, width,...]
    reduce_scatter x1 -> x0, waiting for transfers between devices: 60 us -> none  [per_device(): lax.psum_scatter(jnp.dot(spread, out_weight, preferred_element_type=jnp.f...]
    all_to_all x1 -> x0, blocking collectives: 28.4 us -> none  [per_device(): lax.all_to_all(buffer, 'wide', split_axis=0, concat_axis=0, tiled=True)]
    dot_general x6 -> x0, matrix products: 23.6 us -> none  [the longest x1 9.08 us: per_device(): jnp.einsum('sekd,edf->sekf', slab_in, expert_up, preferred_element_type=j...]
    all_to_all x1 -> x0, waiting for transfers between devices: 22.1 us -> none  [per_device(): lax.all_to_all(processed, 'wide', split_axis=0, concat_axis=0, tiled=True)]
    all_to_all x1 -> x0, starting transfers between devices: 4.99 us -> none  [per_device(): lax.all_to_all(processed, 'wide', split_axis=0, concat_axis=0, tiled=True)]
    convert_element_type x3 -> x0, local copies, waits for them, and re-layouts: 3.34 us -> none  [the longest x1 2.08 us: per_device(): processed = jnp.einsum('sekf,efd->sekd', hidden_mid, expert_down, preferr...]
    all_to_all x1, waiting for transfers between devices: 12.5 us -> 10.5 us  [local_heads(): lax.all_to_all(packed, 'wide', split_axis=2, concat_axis=0, tiled=True)]
  transfers between devices with their start and end apart: 3 -> 1, of which waited for: 3 -> 1; matrix products, arithmetic and copies ran while one was open for 1% -> 3% of each run, Pallas kernels for 0% -> 0%
where the time goes in v1:
time: 106 us; the launch traced here: 105 us
  Pallas kernels  62.6 us (59%)
  local copies, waits for them, and re-layouts  18.4 us (17%)
  waiting for transfers between devices  10.5 us (10%)
  starting transfers between devices  7.36 us (7%)
  matrix products  3.08 us (3%)
  other arithmetic  2.91 us (3%)
    pallas_call x1, Pallas kernels, fused_layer(): pl.pallas_call(functools.partial(layer_kernel, (wide_size, owned, width,...  62.6 us
    all_to_all x1, waiting for transfers between devices, local_heads(): lax.all_to_all(packed, 'wide', split_axis=2, concat_axis=0, tiled=True)  10.5 us
    all_to_all x1, starting transfers between devices, local_heads(): lax.all_to_all(packed, 'wide', split_axis=2, concat_axis=0, tiled=True)  7.36 us
    reshape x6, local copies, waits for them, and re-layouts, by_head(): return array.reshape(owned_req, num_steps, wide_size, -1)  4.79 us
    slice x1, local copies, waits for them, and re-layouts, local_heads(): attended = attended + gram[:, num_steps + t, t][:, None] * now  3.97 us
    dot_general x1, matrix products, local_heads(): jnp.einsum('rsd,rdc->rsc', both, prefill_state, preferred_element_type=jn...  2.84 us
  transfers between devices with their start and end apart: 1, of which 1 were waited for; matrix products, arithmetic and copies ran while one was open for 3% of the time, Pallas kernels for 0%

profile of v1, /device:TPU:0, one launch (start us, length us, event | category | flops | bytes accessed | tf_op | source)
XLA Modules:
  0.0 105.1 jit_solution(6440376124697100673)
XLA Ops:
  0.0 0.9 reshape.219
  0.9 0.9 reshape.220
  1.8 1.0 reshape.221
  2.8 1.0 reshape.222
  3.8 0.8 copy.116
  4.6 0.5 copy.118
  5.1 0.8 copy.117
  5.9 0.5 copy.119
  6.6 1.1 %copy.120 = bf16[4,4,16,772]{3,0,1,2:T(4,128)(2,1)} copy(bf16[4,4,16,772]{3,2,1,0:T(8,128)(2,1)S(1)} %concatenate.10) | data formatting | bytes 790528 | tf_op jit(solution)/shard_map/concatenate | solution.py:47
  7.7 7.4 %all-to-all-start = ((bf16[4,4,16,772]{3,0,1,2:T(4,128)(2,1)}), bf16[4,4,16,772]{3,0,1,2:T(4,128)(2,1)S(1)}, u32[]{:S(2)}, u32[]{:S(2)}) async-start(bf16[4,4,16,772]{3,0,1,2:T(4,128)(2,1)} %copy.120), calls=%async_computation | async-start | bytes 917504 | tf_op jit(solution)/shard_map/all_to_all | solution.py:50
  15.1 1.5 %reshape.229.resid_ref = bf16[16,2048]{1,0:T(8,128)(2,1)} reshape(bf16[4,4,2048]{2,1,0:T(4,128)(2,1)} %param.17) | data formatting | bytes 131072 | tf_op jit(solution)/shard_map/reshape | solution.py:435
  16.6 0.7 convert.5
  17.3 0.6 pad.5.ids_ref
  17.9 10.5 %all-to-all-done = bf16[4,4,16,772]{3,0,1,2:T(4,128)(2,1)S(1)} async-done(((bf16[4,4,16,772]{3,0,1,2:T(4,128)(2,1)}), bf16[4,4,16,772]{3,0,1,2:T(4,128)(2,1)S(1)}, u32[]{:S(2)}, u32[]{:S(2)}) %all-to-all-start) | async-done | bytes 395296 | tf_op jit(solution)/shard_map/all_to_all | solution.py:50
  28.5 0.2 squeeze.2
  29.1 0.2 copy.133
  29.8 0.2 fusion
  30.0 2.8 %fusion.5 = f32[64,8,256]{2,1,0:T(8,128)S(1)} fusion(bf16[64,128,256]{2,1,0:T(8,128)(2,1)} %param.16, bf16[64,8,128]{2,0,1:T(8,128)(2,1)S(1)} %pad_maximum_fusion.1), kind=kOutput, calls=%fused_computation.16 | convolution fusion | flops 33554432 | bytes 4849664 | tf_op jit(solution)/shard_map/rsd,rdc->rsc/dot_general | solution.py:63
  32.8 0.3 broadcast_in_dim.5
  33.2 0.2 reshape.226
  33.4 0.3 broadcast_in_dim.4
  33.8 0.2 reshape.225
  34.0 4.0 %slice_reduce_fusion.15 = (f32[64]{0:T(128)S(1)}, f32[64]{0:T(128)S(1)}, f32[64]{0:T(128)S(1)}, f32[64]{0:T(128)S(1)}, f32[64]{0:T(128)S(1)}, /*index=5*/f32[64]...) fusion(f32[64,8,4]{1,2,0:T(4,128)S(1)} %fusion), kind=kLoop, calls=%fused_computation.74 | loop fusion | bytes 8192 | tf_op jit(solution)/shard_map/slice | solution.py:84
  37.9 0.2 copy_multiply_fusion
  38.7 0.2 copy.129
  39.1 0.2 mul.429
  39.3 0.3 reduce_sum.29
  39.7 0.3 mul.430
  40.0 0.2 mul.431
  40.3 0.7 multiply_convert_fusion.heads_ref
  41.0 62.6 %shard_map.154 = bf16[16,2048]{1,0:T(8,128)(2,1)} custom-call(bf16[8,2,16,256]{3,2,1,0:T(8,128)(2,1)} %multiply_convert_fusion.heads_ref, bf16[256,2048]{1,0:T(8,128)(2,1)} %out_w_ref.1, bf16[16,2048]{1,0:T(8,128)(2,1)} %reshape.229.resid_ref, f32[1,2048]{1,0:T(1,128)} %bitcast.20, bf16[2048,128]{1,0:T(8,128)(2,1)} %router_ref.1, ...), custom_call_target="tpu_custom_call" | custom-call | tf_op jit(solution)/shard_map/pallas_call | solution.py:398
  103.6 1.5 %reshape.232 = bf16[4,4,2048]{2,1,0:T(4,128)(2,1)} reshape(bf16[16,2048]{1,0:T(8,128)(2,1)} %shard_map.154) | data formatting | bytes 131072 | tf_op jit(solution)/shard_map/reshape | solution.py:443
  (25 shorter events, 1.9 us)
Async XLA Ops:
  0.0 17.8 %copy-start = (f32[128]{0:T(128)S(1)}, f32[128]{0:T(128)}, u32[]{:S(2)}) copy-start(f32[128]{0:T(128)} %param.24) | copy-start | bytes 1540
  7.7 20.6 %all-to-all-start = ((bf16[4,4,16,772]{3,0,1,2:T(4,128)(2,1)}), bf16[4,4,16,772]{3,0,1,2:T(4,128)(2,1)S(1)}, u32[]{:S(2)}, u32[]{:S(2)}) async-start(bf16[4,4,16,772]{3,0,1,2:T(4,128)(2,1)} %copy.120), calls=%async_computation | async-start | bytes 917504 | tf_op jit(solution)/shard_map/all_to_all | solution.py:50

commit v2 on v1

--- a/solution.py
+++ b/solution.py
@@ -144,16 +144,26 @@
 
 def layer_kernel(
     sizes,
-    heads_ref,
+    state_hbm,
+    q_ref,
+    k_ref,
+    v_ref,
+    g_ref,
+    facts_ref,
+    gain_ref,
     out_w_ref,
     resid_ref,
     post_ref,
     router_ref,
-    ids_ref,
     gate_hbm,
     up_hbm,
     down_hbm,
     mixed_ref,
+    state,
+    outbox,
+    inbox,
+    from_state,
+    heads,
     gate_w,
     up_w,
     down_w,
@@ -171,6 +181,9 @@
     outcome,
     pick_hi,
     pick_lo,
+    state_sem,
+    box_send_sem,
+    box_recv_sem,
     w_sem,
     rs_send_sem,
     rs_recv_sem,
@@ -205,16 +218,41 @@
             for i, (hbm, vmem) in enumerate(((gate_hbm, gate_w), (up_hbm, up_w), (down_hbm, down_w)))
         ]
 
+    state_copy = pltpu.make_async_copy(state_hbm, state, state_sem)
+    state_copy.start()
     for e in range(held):
         for copy in weight_copies(e, e):
             copy.start()
 
     barrier = pltpu.get_barrier_semaphore()
-    for mate in [core_mate, x_mate] + z_mates:
+    moves = [(dz, dx, dc) for dz in range(num_z) for dx in range(2) for dc in range(2)][1:]
+
+    def offset(at_z, dx, dc):
+        return device_at(at_z, 1 - x if dx else x, 1 - core if dc else core)
+
+    for dz, dx, dc in moves:
+        mate = offset(z_ahead(dz), dx, dc)
         pl.semaphore_signal(
             barrier, inc=1, device_id={"wide": mate}, device_id_type=pl.DeviceIdType.MESH
         )
-    pl.semaphore_wait(barrier, 1 + num_z)
+    requests, num_steps, _ = q_ref.shape
+
+    def flat(ref):
+        return jnp.concatenate([ref[r].astype(jnp.float32) for r in range(requests)], axis=0)
+
+    fields = []
+    for ref in (q_ref, k_ref, v_ref, g_ref):
+        values = flat(ref).astype(jnp.bfloat16)
+        size = values.shape[1] // wide_size
+        at = sum(fields)
+        for to in range(wide_size):
+            outbox[to, :, at : at + size] = values[:, to * size : (to + 1) * size]
+        fields.append(size)
+    key_dim, columns = fields[0], fields[2]
+    values_at, gate_at, facts_at = 2 * key_dim, 2 * key_dim + columns, sum(fields)
+    for to in range(wide_size):
+        outbox[to, :, facts_at:] = facts_ref[...]
+    pl.semaphore_wait(barrier, wide_size - 1)
 
     def remote(src, dst, send_sem, recv_sem, mate):
         return pltpu.make_async_remote_copy(
@@ -225,6 +263,100 @@
             device_id={"wide": mate},
             device_id_type=pl.DeviceIdType.MESH,
         )
+
+    posted = []
+    for i in reversed(range(len(moves))):
+        dz, dx, dc = moves[i]
+        mate = offset(z_ahead(dz), dx, dc)
+        copy = remote(
+            outbox.at[mate], inbox.at[me], box_send_sem.at[i], box_recv_sem.at[i], mate
+        )
+        copy.start()
+        posted.insert(0, copy)
+    inbox[me] = outbox[me]
+    state_copy.wait()
+    of_request = lax.broadcasted_iota(jnp.int32, (2 * owned, requests * key_dim), 0) % owned
+    of_lane = lax.broadcasted_iota(jnp.int32, (2 * owned, requests * key_dim), 1)
+    own_state = jnp.where(of_request // num_steps == of_lane // key_dim, 1.0, 0.0)
+    own_state = own_state.astype(jnp.bfloat16)
+
+    def meet_state(block):
+        came = inbox[block]
+        pair = jnp.concatenate([came[:, key_dim : 2 * key_dim], came[:, :key_dim]], axis=0)
+        spaced = jnp.concatenate([pair] * requests, axis=1) * own_state
+        from_state[block] = dot(spaced, state[block])
+
+    meet_state(me)
+    for i, (dz, dx, dc) in enumerate(moves):
+        posted[i].wait_recv()
+        meet_state(offset(z_behind(dz), dx, dc))
+
+    at_once = 4
+    many = at_once * owned
+    head_dim = gain_ref.shape[1]
+    group = columns // head_dim
+    value_heads = group * wide_size
+    step = lax.broadcasted_iota(jnp.int32, (many, head_dim), 0) % num_steps
+    step_col = step[:, :1]
+    lane = lax.broadcasted_iota(jnp.int32, (many, 128), 1)
+
+    def unit(vectors):
+        return lax.rsqrt(jnp.sum(vectors * vectors, axis=1, keepdims=True) + 1e-06)
+
+    def before(array, d):
+        return pltpu.roll(array, d, 0) if d else array
+
+    for first in range(0, wide_size, at_once):
+        came = inbox[first : first + at_once].reshape(many, inbox.shape[-1])
+        q_raw = came[:, :key_dim].astype(jnp.float32)
+        k_raw = came[:, key_dim : 2 * key_dim].astype(jnp.float32)
+        q_inv, k_inv = unit(q_raw), unit(k_raw)
+        q_unit, k_unit = q_raw * q_inv, k_raw * k_inv
+        met = from_state[first : first + at_once]
+        k_met = met[:, :owned].reshape(many, columns) * k_inv
+        q_met = met[:, owned:].reshape(many, columns) * q_inv
+        kk, qk = [], []
+        for d in range(num_steps):
+            earlier = before(k_unit, d)
+            valid = step_col >= d
+            kk.append(
+                jnp.where(valid, jnp.sum(k_unit * earlier, axis=1, keepdims=True), 0.0)
+            )
+            qk.append(
+                jnp.where(valid, jnp.sum(q_unit * earlier, axis=1, keepdims=True), 0.0)
+            )
+        facts = came[:, facts_at:].astype(jnp.float32)
+        for j in range(group):
+            cut = slice(j * head_dim, (j + 1) * head_dim)
+            head = me * group + j
+            beta = jnp.sum(jnp.where(lane == head, facts, 0.0), axis=1, keepdims=True)
+            decay = jnp.sum(
+                jnp.where(lane == head + value_heads, facts, 0.0), axis=1, keepdims=True
+            )
+            decay = jnp.broadcast_to(decay, (many, head_dim))
+            kept = [None, decay]
+            for d in range(1, num_steps):
+                kept.append(kept[d] * before(decay, d))
+            through = decay
+            for t in range(1, num_steps):
+                through = jnp.where(step == t, kept[t + 1], through)
+            value_cols = came[:, values_at:gate_at][:, cut].astype(jnp.float32)
+            base = value_cols - through * k_met[:, cut]
+            change = beta * base
+            for _ in range(1, num_steps):
+                rest = base
+                for d in range(1, num_steps):
+                    rest = rest - kept[d] * kk[d] * before(change, d)
+                change = beta * rest
+            attended = through * q_met[:, cut] + qk[0] * change
+            for d in range(1, num_steps):
+                attended = attended + kept[d] * qk[d] * before(change, d)
+            scale = lax.rsqrt(jnp.mean(attended * attended, axis=1, keepdims=True) + 1e-06)
+            gate_act = jax.nn.silu(came[:, gate_at:facts_at][:, cut].astype(jnp.float32))
+            normed = (attended * scale * gain_ref[...] * gate_act).astype(jnp.bfloat16)
+            heads[first // 2 : (first + at_once) // 2, :, :, cut] = normed.reshape(
+                at_once // 2, 2, owned, head_dim
+            )
 
     def reduce_scatter(turn, produce):
         def exchange(i, src, dst, mate):
@@ -258,13 +390,12 @@
         return total
 
     def project(at_core):
-        return dot(heads_ref[:, at_core].reshape(half, heads_ref.shape[-1]), out_w_ref[...])
-
-    now = resid_ref[...].astype(jnp.float32) + reduce_scatter(0, project)
+        return dot(heads[:, at_core].reshape(half, columns), out_w_ref[...])
+
+    now = flat(resid_ref) + reduce_scatter(0, project)
     hidden[...] = now
     moe_in = now * lax.rsqrt(jnp.mean(now * now, axis=-1, keepdims=True) + 1e-06) * post_ref[...]
-    tokens[me, :, :width] = moe_in.astype(jnp.bfloat16)
-    tokens[me, :, width:] = ids_ref[...]
+    tokens[me] = moe_in.astype(jnp.bfloat16)
 
     sent = []
 
@@ -302,18 +433,18 @@
     for at_z in range(num_z):
         for at_x in range(2):
             arrived(device_at(at_z, at_x, 1 - core), core_mate)
-    for copy in sent:
+    for copy in posted + sent:
         copy.wait_send()
 
-    everyone = tokens[...].reshape(rows, width + 128)
-    all_in = everyone[:, :width]
-    named = everyone[:, width:].astype(jnp.float32)
+    all_in = tokens[...].reshape(rows, width)
+    named = inbox[:, :, facts_at:].reshape(rows, 128).astype(jnp.float32)
     logits = dot(all_in, router_ref[...])
     lanes = lax.broadcasted_iota(jnp.int32, (rows, experts), 1).astype(jnp.float32)
     squashed = jnp.zeros((rows, experts), jnp.float32)
     chosen = jnp.zeros((rows, experts), jnp.float32)
+    ids_at = 2 * value_heads
     for k in range(TOPK):
-        chosen = jnp.where(named[:, k : k + 1] == lanes, 1.0, chosen)
+        chosen = jnp.where(named[:, ids_at + k : ids_at + k + 1] == lanes, 1.0, chosen)
     squashed = jnp.where(chosen > 0.5, jax.nn.sigmoid(logits), 0.0)
     gates = squashed / jnp.sum(squashed, axis=1, keepdims=True)
     gates_hi = gates.astype(jnp.bfloat16)
@@ -372,25 +503,45 @@
         lo = pick_lo[:, at_core].reshape(half, local_experts * slots)
         return dot(hi, results) + dot(lo, results)
 
-    mixed_ref[...] = (reduce_scatter(1, combine) + hidden[...]).astype(mixed_ref.dtype)
+    result = reduce_scatter(1, combine) + hidden[...]
+    for r in range(requests):
+        mixed_ref[r] = result[r * num_steps : (r + 1) * num_steps].astype(mixed_ref.dtype)
 
 
 def fused_layer(
-    spread, residual_in, out_weight, post_gain, router_weight, expert_ids, expert_gate, expert_up, expert_down
+    prefill_state,
+    residual_in,
+    queries,
+    keys_in,
+    values_in,
+    gate_in,
+    beta_rate,
+    decay_rate,
+    norm_gain,
+    out_weight,
+    post_gain,
+    router_weight,
+    expert_ids,
+    expert_gate,
+    expert_up,
+    expert_down,
 ):
     wide_size = lax.axis_size("wide")
     owned_req, num_steps, width = residual_in.shape
     owned = owned_req * num_steps
     rows = wide_size * owned
-    columns = spread.shape[1]
+    total_req, key_dim, columns = prefill_state.shape
+    value_heads = beta_rate.shape[2]
+    box = 2 * key_dim + 2 * columns + 128
     num_z = wide_size // 4
     experts = router_weight.shape[1]
     local_experts, _, hidden_units = expert_gate.shape
     held = min(local_experts, 6)
     slots = CAP * wide_size
-    ids = jnp.pad(
-        expert_ids.reshape(owned, TOPK), ((0, 0), (0, 128 - TOPK)), constant_values=-1
-    ).astype(jnp.bfloat16)
+    facts = jnp.concatenate(
+        [beta_rate, decay_rate, expert_ids.astype(jnp.bfloat16)], axis=-1
+    ).reshape(owned, 2 * value_heads + TOPK)
+    facts = jnp.pad(facts, ((0, 0), (0, 128 - facts.shape[1])))
     half16 = (2, num_z, 2, owned, width)
     bf16, f32 = jnp.bfloat16, jnp.float32
     vmem = pl.BlockSpec(memory_space=pltpu.VMEM)
@@ -399,10 +550,15 @@
         functools.partial(
             layer_kernel, (wide_size, owned, width, experts, local_experts, held)
         ),
-        out_shape=jax.ShapeDtypeStruct((owned, width), bf16),
-        in_specs=[vmem] * 6 + [hbm] * 3,
+        out_shape=jax.ShapeDtypeStruct((owned_req, num_steps, width), bf16),
+        in_specs=[hbm] + [vmem] * 10 + [hbm] * 3,
         out_specs=vmem,
         scratch_shapes=[
+            pltpu.VMEM((wide_size, owned_req * key_dim, columns), bf16),
+            pltpu.VMEM((wide_size, owned, box), bf16),
+            pltpu.VMEM((wide_size, owned, box), bf16),
+            pltpu.VMEM((wide_size, 2 * owned, columns), f32),
+            pltpu.VMEM((num_z * 2, 2, owned, columns), bf16),
             pltpu.VMEM((held, width, hidden_units), bf16),
             pltpu.VMEM((held, width, hidden_units), bf16),
             pltpu.VMEM((held, hidden_units, width), bf16),
@@ -415,11 +571,14 @@
             pltpu.VMEM((num_z, 2, owned, width), f32),
             pltpu.VMEM((num_z, owned, width), f32),
             pltpu.VMEM((owned, width), f32),
-            pltpu.VMEM((wide_size, owned, width + 128), bf16),
+            pltpu.VMEM((wide_size, owned, width), bf16),
             pltpu.VMEM((local_experts, slots, width), bf16),
             pltpu.VMEM((local_experts, slots, width), bf16),
             pltpu.VMEM((num_z * 2, 2, owned, local_experts * slots), bf16),
             pltpu.VMEM((num_z * 2, 2, owned, local_experts * slots), bf16),
+            pltpu.SemaphoreType.DMA,
+            pltpu.SemaphoreType.DMA((wide_size - 1,)),
+            pltpu.SemaphoreType.DMA((wide_size - 1,)),
             pltpu.SemaphoreType.DMA((3, held)),
             pltpu.SemaphoreType.DMA((2, 1 + num_z)),
             pltpu.SemaphoreType.DMA((2, 1 + num_z)),
@@ -430,17 +589,22 @@
             collective_id=0, has_side_effects=True, vmem_limit_bytes=60 * 1024 * 1024
         ),
     )(
-        spread.reshape(num_z * 2, 2, owned, columns),
+        prefill_state.reshape(wide_size, owned_req * key_dim, columns),
+        queries,
+        keys_in,
+        values_in,
+        gate_in,
+        facts,
+        norm_gain.reshape(1, norm_gain.shape[0]),
         out_weight,
-        residual_in.reshape(owned, width),
+        residual_in,
         post_gain.reshape(1, width),
         router_weight,
-        ids,
         expert_gate,
         expert_up,
         expert_down,
     )
-    return out.reshape(owned_req, num_steps, width)
+    return out
 
 
 def per_device(
@@ -473,14 +637,17 @@
     key_heads = queries.shape[2] // key_dim
     key_group = hv_dv // key_heads
     width = residual_in.shape[2]
-    heads = local_heads if key_heads == wide_size else moved_heads
-    spread = heads(
-        prefill_state, queries, keys_in, values_in, gate_in, beta_rate, decay_rate, norm_gain
-    )
     if key_heads == wide_size == 16 and local_rows == 16 and router_weight.shape[1] == 128:
         return fused_layer(
-            spread,
+            prefill_state,
             residual_in,
+            queries,
+            keys_in,
+            values_in,
+            gate_in,
+            beta_rate,
+            decay_rate,
+            norm_gain,
             out_weight,
             post_gain,
             router_weight,
@@ -489,6 +656,10 @@
             expert_up,
             expert_down,
         )
+    heads = local_heads if key_heads == wide_size else moved_heads
+    spread = heads(
+        prefill_state, queries, keys_in, values_in, gate_in, beta_rate, decay_rate, norm_gain
+    )
     attention = lax.psum_scatter(
         jnp.dot(spread, out_weight, preferred_element_type=jnp.float32),
         "wide",

time: 106 us -> 85.1 us (0.80)
  Pallas kernels: 62.6 us -> 81.3 us
  local copies, waits for them, and re-layouts: 18.4 us -> 2.09 us
  waiting for transfers between devices: 10.5 us -> 0 us
  starting transfers between devices: 7.36 us -> 0 us
  matrix products: 3.08 us -> 0 us
  other arithmetic: 2.91 us -> 1.48 us
    pallas_call x1, Pallas kernels: 62.6 us -> 81.3 us  [fused_layer(): pl.pallas_call(functools.partial(layer_kernel, (wide_size, owned, width,...]
    all_to_all x1 -> x0, waiting for transfers between devices: 10.5 us -> none  [local_heads(): lax.all_to_all(packed, 'wide', split_axis=2, concat_axis=0, tiled=True)]
    reshape x12 -> x0, local copies, waits for them, and re-layouts: 8.38 us -> none  [the longest x6 4.79 us: by_head(): return array.reshape(owned_req, num_steps, wide_size, -1)]
    all_to_all x1 -> x0, starting transfers between devices: 7.36 us -> none  [local_heads(): lax.all_to_all(packed, 'wide', split_axis=2, concat_axis=0, tiled=True)]
    slice x1 -> x0, local copies, waits for them, and re-layouts: 3.97 us -> none  [local_heads(): attended = attended + gram[:, num_steps + t, t][:, None] * now]
    dot_general x2 -> x0, matrix products: 3.08 us -> none  [the longest x1 2.84 us: local_heads(): jnp.einsum('rsd,rdc->rsc', both, prefill_state, preferred_element_type=jn...]
    concatenate x3 -> x0, local copies, waits for them, and re-layouts: 1.33 us -> none  [the longest x2 1.27 us: local_heads(): jnp.concatenate([by_head(a) for a in (queries, keys_in, values_in, gate_i...]
    mul x6 -> x0, local copies, waits for them, and re-layouts: 1.09 us -> none  [the longest x3 0.55 us: local_heads(): normed = (heads_view * scale * norm_gain * gate_act).astype(jnp.bfloat16)]
  transfers between devices with their start and end apart: 1 -> 0, of which waited for: 1 -> 0; matrix products, arithmetic and copies ran while one was open for 3% -> 0% of each run, Pallas kernels for 0% -> 0%
where the time goes in v2:
time: 85.1 us; the launch traced here: 84.8 us
  Pallas kernels  81.3 us (96%)
  local copies, waits for them, and re-layouts  2.09 us (2%)
  other arithmetic  1.48 us (2%)
    pallas_call x1, Pallas kernels, fused_layer(): pl.pallas_call(functools.partial(layer_kernel, (wide_size, owned, width,...  81.3 us

profile of v2, /device:TPU:0, one launch (start us, length us, event | category | flops | bytes accessed | tf_op | source)
XLA Modules:
  0.0 84.8 jit_solution(8248330563121579192)
XLA Ops:
  0.0 0.7 convert_element_type.5
  0.7 0.8 pad_maximum_fusion
  1.5 0.6 pad.4.facts_ref
  2.1 81.3 %shard_map.154 = bf16[4,4,2048]{2,1,0:T(4,128)(2,1)} custom-call(bf16[16,512,256]{2,1,0:T(8,128)(2,1)} %bitcast.4, bf16[4,4,2048]{2,1,0:T(4,128)(2,1)} %q_ref.1, bf16[4,4,2048]{2,1,0:T(4,128)(2,1)} %k_ref.1, bf16[4,4,4096]{2,1,0:T(4,128)(2,1)} %v_ref.1, bf16[4,4,4096]{2,1,0:T(4,128)(2,1)} %g_ref.1, bf16[16,128]{1,0:T(8,128)(2,1)} %pad.4.facts_ref, ...), custom_call_target="tpu_custom_call" | custom-call | tf_op jit(solution)/shard_map/pallas_call | solution.py:549
  83.3 1.5 %copy.18 = bf16[4,4,2048]{2,1,0:T(4,128)(2,1)} copy(bf16[4,4,2048]{2,1,0:T(4,128)(2,1)} %shard_map.154) | data formatting | bytes 131072

commit v3 on v2

--- a/solution.py
+++ b/solution.py
@@ -178,19 +178,20 @@
     hidden,
     tokens,
     slab,
-    outcome,
+    mid,
     pick_hi,
     pick_lo,
     state_sem,
     box_send_sem,
     box_recv_sem,
     w_sem,
+    down_sem,
     rs_send_sem,
     rs_recv_sem,
     ag_send_sem,
     ag_recv_sem,
 ):
-    wide_size, owned, width, experts, local_experts, held = sizes
+    wide_size, owned, width, experts, local_experts, held, chunks = sizes
     num_z = wide_size // 4
     rows = wide_size * owned
     half = rows // 2
@@ -212,18 +213,17 @@
     x_mate = device_at(z, 1 - x, core)
     z_mates = [device_at(z_ahead(d), x, core) for d in range(1, num_z)]
 
-    def weight_copies(e, slot):
+    def up_copies(e, slot):
         return [
             pltpu.make_async_copy(hbm.at[e], vmem.at[slot], w_sem.at[i, slot])
-            for i, (hbm, vmem) in enumerate(((gate_hbm, gate_w), (up_hbm, up_w), (down_hbm, down_w)))
+            for i, (hbm, vmem) in enumerate(((gate_hbm, gate_w), (up_hbm, up_w)))
         ]
+
+    def down_copy(e):
+        return pltpu.make_async_copy(down_hbm.at[e], down_w.at[e], down_sem.at[e])
 
     state_copy = pltpu.make_async_copy(state_hbm, state, state_sem)
     state_copy.start()
-    for e in range(held):
-        for copy in weight_copies(e, e):
-            copy.start()
-
     barrier = pltpu.get_barrier_semaphore()
     moves = [(dz, dx, dc) for dz in range(num_z) for dx in range(2) for dc in range(2)][1:]
 
@@ -290,6 +290,12 @@
     for i, (dz, dx, dc) in enumerate(moves):
         posted[i].wait_recv()
         meet_state(offset(z_behind(dz), dx, dc))
+
+    for e in range(held):
+        for copy in up_copies(e, e):
+            copy.start()
+    for e in range(local_experts):
+        down_copy(e).start()
 
     at_once = 4
     many = at_once * owned
@@ -358,39 +364,64 @@
                 at_once // 2, 2, owned, head_dim
             )
 
+    wide_cut = width // chunks
+
     def reduce_scatter(turn, produce):
-        def exchange(i, src, dst, mate):
-            copy = remote(src, dst, rs_send_sem.at[turn, i], rs_recv_sem.at[turn, i], mate)
+        started = {}
+
+        def exchange(c, i, src, dst, mate):
+            copy = remote(src, dst, rs_send_sem.at[turn, c, i], rs_recv_sem.at[turn, c, i], mate)
             copy.start()
-            return copy
-
-        core_send[turn] = produce(1 - core).astype(jnp.bfloat16).reshape(num_z, 2, owned, width)
-        to_core = exchange(0, core_send.at[turn], core_recv.at[turn], core_mate)
-        part[...] = produce(core).reshape(num_z, 2, owned, width)
-        to_core.wait()
-        x_send[turn] = (part[:, 1 - x] + core_recv[turn, :, 1 - x].astype(jnp.float32)).astype(
-            jnp.bfloat16
-        )
-        to_x = exchange(1, x_send.at[turn], x_recv.at[turn], x_mate)
-        lane_part[...] = part[:, x] + core_recv[turn, :, x].astype(jnp.float32)
-        to_x.wait()
-        to_z = []
-        for d in range(1, num_z):
-            at_z = z_ahead(d)
-            z_send[turn, d - 1] = (
-                lane_part[at_z] + x_recv[turn, at_z].astype(jnp.float32)
+            started[c, i] = copy
+
+        def over_cores(c):
+            sums = produce(c)
+            core_send[turn, c] = (
+                sums(1 - core).astype(jnp.bfloat16).reshape(num_z, 2, owned, wide_cut)
+            )
+            exchange(c, 0, core_send.at[turn, c], core_recv.at[turn, c], core_mate)
+            part[c] = sums(core).reshape(num_z, 2, owned, wide_cut)
+
+        def over_x(c):
+            started[c, 0].wait_recv()
+            x_send[turn, c] = (
+                part[c, :, 1 - x] + core_recv[turn, c, :, 1 - x].astype(jnp.float32)
             ).astype(jnp.bfloat16)
-            to_z.append(
-                exchange(1 + d, z_send.at[turn, d - 1], z_recv.at[turn, d - 1], z_mates[d - 1])
-            )
-        total = lane_part[z] + x_recv[turn, z].astype(jnp.float32)
-        for d in range(1, num_z):
-            to_z[d - 1].wait()
-            total = total + z_recv[turn, d - 1].astype(jnp.float32)
-        return total
-
-    def project(at_core):
-        return dot(heads[:, at_core].reshape(half, columns), out_w_ref[...])
+            exchange(c, 1, x_send.at[turn, c], x_recv.at[turn, c], x_mate)
+            lane_part[c] = part[c, :, x] + core_recv[turn, c, :, x].astype(jnp.float32)
+
+        def over_z(c):
+            started[c, 1].wait_recv()
+            for d in range(1, num_z):
+                at_z = z_ahead(d)
+                z_send[turn, c, d - 1] = (
+                    lane_part[c, at_z] + x_recv[turn, c, at_z].astype(jnp.float32)
+                ).astype(jnp.bfloat16)
+                exchange(
+                    c, 1 + d, z_send.at[turn, c, d - 1], z_recv.at[turn, c, d - 1], z_mates[d - 1]
+                )
+
+        def total(c):
+            value = lane_part[c, z] + x_recv[turn, c, z].astype(jnp.float32)
+            for d in range(1, num_z):
+                started[c, 1 + d].wait_recv()
+                value = value + z_recv[turn, c, d - 1].astype(jnp.float32)
+            return value
+
+        totals = []
+        for tick in range(chunks + 3):
+            for late, stage in enumerate((over_cores, over_x, over_z)):
+                if 0 <= tick - late < chunks:
+                    stage(tick - late)
+            if tick >= 3:
+                totals.append(total(tick - 3))
+        for copy in started.values():
+            copy.wait_send()
+        return jnp.concatenate(totals, axis=1)
+
+    def project(c):
+        weights = out_w_ref[:, c * wide_cut : (c + 1) * wide_cut]
+        return lambda at_core: dot(heads[:, at_core].reshape(half, columns), weights)
 
     now = flat(resid_ref) + reduce_scatter(0, project)
     hidden[...] = now
@@ -484,24 +515,34 @@
     @pl.loop(0, local_experts)
     def _(e):
         slot = lax.rem(e, held)
-        for copy in weight_copies(e, slot):
+        for copy in up_copies(e, slot):
             copy.wait()
         came = slab[e]
         gate_part = dot(came, gate_w[slot])
         up_part = dot(came, up_w[slot])
-        mid = (jax.nn.silu(gate_part) * up_part).astype(jnp.bfloat16)
-        outcome[e] = dot(mid, down_w[slot]).astype(jnp.bfloat16)
+        mid[e] = (jax.nn.silu(gate_part) * up_part).astype(jnp.bfloat16)
 
         @pl.when(e + held < local_experts)
         def _():
-            for copy in weight_copies(e + held, slot):
+            for copy in up_copies(e + held, slot):
                 copy.start()
 
-    def combine(at_core):
-        results = outcome[...].reshape(local_experts * slots, width)
-        hi = pick_hi[:, at_core].reshape(half, local_experts * slots)
-        lo = pick_lo[:, at_core].reshape(half, local_experts * slots)
-        return dot(hi, results) + dot(lo, results)
+    for e in range(local_experts):
+        down_copy(e).wait()
+
+    def combine(c):
+        cut = slice(c * wide_cut, (c + 1) * wide_cut)
+        results = jnp.concatenate(
+            [dot(mid[e], down_w[e, :, cut]).astype(jnp.bfloat16) for e in range(local_experts)],
+            axis=0,
+        )
+
+        def sums(at_core):
+            hi = pick_hi[:, at_core].reshape(half, local_experts * slots)
+            lo = pick_lo[:, at_core].reshape(half, local_experts * slots)
+            return dot(hi, results) + dot(lo, results)
+
+        return sums
 
     result = reduce_scatter(1, combine) + hidden[...]
     for r in range(requests):
@@ -542,13 +583,15 @@
         [beta_rate, decay_rate, expert_ids.astype(jnp.bfloat16)], axis=-1
     ).reshape(owned, 2 * value_heads + TOPK)
     facts = jnp.pad(facts, ((0, 0), (0, 128 - facts.shape[1])))
-    half16 = (2, num_z, 2, owned, width)
+    chunks = 4
+    cut = width // chunks
+    half16 = (2, chunks, num_z, 2, owned, cut)
     bf16, f32 = jnp.bfloat16, jnp.float32
     vmem = pl.BlockSpec(memory_space=pltpu.VMEM)
     hbm = pl.BlockSpec(memory_space=pl.ANY)
     out = pl.pallas_call(
         functools.partial(
-            layer_kernel, (wide_size, owned, width, experts, local_experts, held)
+            layer_kernel, (wide_size, owned, width, experts, local_experts, held, chunks)
         ),
         out_shape=jax.ShapeDtypeStruct((owned_req, num_steps, width), bf16),
         in_specs=[hbm] + [vmem] * 10 + [hbm] * 3,
@@ -561,32 +604,33 @@
             pltpu.VMEM((num_z * 2, 2, owned, columns), bf16),
             pltpu.VMEM((held, width, hidden_units), bf16),
             pltpu.VMEM((held, width, hidden_units), bf16),
-            pltpu.VMEM((held, hidden_units, width), bf16),
+            pltpu.VMEM((local_experts, hidden_units, width), bf16),
             pltpu.VMEM(half16, bf16),
             pltpu.VMEM(half16, bf16),
-            pltpu.VMEM((2, num_z, owned, width), bf16),
-            pltpu.VMEM((2, num_z, owned, width), bf16),
-            pltpu.VMEM((2, num_z - 1, owned, width), bf16),
-            pltpu.VMEM((2, num_z - 1, owned, width), bf16),
-            pltpu.VMEM((num_z, 2, owned, width), f32),
-            pltpu.VMEM((num_z, owned, width), f32),
+            pltpu.VMEM((2, chunks, num_z, owned, cut), bf16),
+            pltpu.VMEM((2, chunks, num_z, owned, cut), bf16),
+            pltpu.VMEM((2, chunks, num_z - 1, owned, cut), bf16),
+            pltpu.VMEM((2, chunks, num_z - 1, owned, cut), bf16),
+            pltpu.VMEM((chunks, num_z, 2, owned, cut), f32),
+            pltpu.VMEM((chunks, num_z, owned, cut), f32),
             pltpu.VMEM((owned, width), f32),
             pltpu.VMEM((wide_size, owned, width), bf16),
             pltpu.VMEM((local_experts, slots, width), bf16),
-            pltpu.VMEM((local_experts, slots, width), bf16),
+            pltpu.VMEM((local_experts, slots, hidden_units), bf16),
             pltpu.VMEM((num_z * 2, 2, owned, local_experts * slots), bf16),
             pltpu.VMEM((num_z * 2, 2, owned, local_experts * slots), bf16),
             pltpu.SemaphoreType.DMA,
             pltpu.SemaphoreType.DMA((wide_size - 1,)),
             pltpu.SemaphoreType.DMA((wide_size - 1,)),
-            pltpu.SemaphoreType.DMA((3, held)),
-            pltpu.SemaphoreType.DMA((2, 1 + num_z)),
-            pltpu.SemaphoreType.DMA((2, 1 + num_z)),
+            pltpu.SemaphoreType.DMA((2, held)),
+            pltpu.SemaphoreType.DMA((local_experts,)),
+            pltpu.SemaphoreType.DMA((2, chunks, 1 + num_z)),
+            pltpu.SemaphoreType.DMA((2, chunks, 1 + num_z)),
             pltpu.SemaphoreType.DMA((wide_size,)),
             pltpu.SemaphoreType.DMA((wide_size,)),
         ],
         compiler_params=pltpu.CompilerParams(
-            collective_id=0, has_side_effects=True, vmem_limit_bytes=60 * 1024 * 1024
+            collective_id=0, has_side_effects=True, vmem_limit_bytes=62 * 1024 * 1024
         ),
     )(
         prefill_state.reshape(wide_size, owned_req * key_dim, columns),

time: 85.1 us -> 77.6 us (0.912)
  Pallas kernels: 81.3 us -> 73.8 us
    pallas_call x1, Pallas kernels: 81.3 us -> 73.8 us  [fused_layer(): pl.pallas_call(functools.partial(layer_kernel, (wide_size, owned, width,...]
where the time goes in v3:
time: 77.6 us; the launch traced here: 77.4 us
  Pallas kernels  73.8 us (95%)
  local copies, waits for them, and re-layouts  2.09 us (3%)
  other arithmetic  1.48 us (2%)
    pallas_call x1, Pallas kernels, fused_layer(): pl.pallas_call(functools.partial(layer_kernel, (wide_size, owned, width,...  73.8 us

profile of v3, /device:TPU:0, one launch (start us, length us, event | category | flops | bytes accessed | tf_op | source)
XLA Modules:
  0.0 77.4 jit_solution(12222296028015631606)
XLA Ops:
  0.0 0.7 convert_element_type.5
  0.7 0.8 %pad_maximum_fusion = bf16[4,4,74]{2,1,0:T(4,128)(2,1)S(1)} fusion(bf16[4,4,10]{2,1,0:T(4,128)(2,1)S(1)} %convert_element_type.5, bf16[4,4,32]{2,1,0:T(4,128)(2,1)} %param.23, bf16[4,4,32]{2,1,0:T(4,128)(2,1)} %param.22), kind=kLoop, calls=%fused_computation | loop fusion | flops 7104 | bytes 4736 | tf_op jit(solution)/shard_map/concatenate | solution.py:582
  1.5 0.6 pad.4.facts_ref
  2.1 73.8 %shard_map.154 = bf16[4,4,2048]{2,1,0:T(4,128)(2,1)} custom-call(bf16[16,512,256]{2,1,0:T(8,128)(2,1)} %bitcast.4, bf16[4,4,2048]{2,1,0:T(4,128)(2,1)} %q_ref.1, bf16[4,4,2048]{2,1,0:T(4,128)(2,1)} %k_ref.1, bf16[4,4,4096]{2,1,0:T(4,128)(2,1)} %v_ref.1, bf16[4,4,4096]{2,1,0:T(4,128)(2,1)} %g_ref.1, bf16[16,128]{1,0:T(8,128)(2,1)} %pad.4.facts_ref, ...), custom_call_target="tpu_custom_call" | custom-call | tf_op jit(solution)/shard_map/pallas_call | solution.py:592
  75.9 1.5 %copy.18 = bf16[4,4,2048]{2,1,0:T(4,128)(2,1)} copy(bf16[4,4,2048]{2,1,0:T(4,128)(2,1)} %shard_map.154) | data formatting | bytes 131072

commit v4 on v3

--- a/solution.py
+++ b/solution.py
@@ -145,20 +145,27 @@
 def layer_kernel(
     sizes,
     state_hbm,
+    q_hbm,
+    k_hbm,
+    v_hbm,
+    g_hbm,
+    facts_ref,
+    gain_ref,
+    out_w_hbm,
+    resid_hbm,
+    post_ref,
+    router_hbm,
+    gate_hbm,
+    up_hbm,
+    down_hbm,
+    mixed_ref,
     q_ref,
     k_ref,
     v_ref,
     g_ref,
-    facts_ref,
-    gain_ref,
     out_w_ref,
     resid_ref,
-    post_ref,
     router_ref,
-    gate_hbm,
-    up_hbm,
-    down_hbm,
-    mixed_ref,
     state,
     outbox,
     inbox,
@@ -181,6 +188,7 @@
     mid,
     pick_hi,
     pick_lo,
+    early_sem,
     state_sem,
     box_send_sem,
     box_recv_sem,
@@ -222,6 +230,22 @@
     def down_copy(e):
         return pltpu.make_async_copy(down_hbm.at[e], down_w.at[e], down_sem.at[e])
 
+    early = [
+        pltpu.make_async_copy(source, held_here, early_sem.at[i])
+        for i, (source, held_here) in enumerate(
+            (
+                (q_hbm, q_ref),
+                (k_hbm, k_ref),
+                (v_hbm, v_ref),
+                (g_hbm, g_ref),
+                (out_w_hbm, out_w_ref),
+                (resid_hbm, resid_ref),
+                (router_hbm, router_ref),
+            )
+        )
+    ]
+    for copy in early:
+        copy.start()
     state_copy = pltpu.make_async_copy(state_hbm, state, state_sem)
     state_copy.start()
     barrier = pltpu.get_barrier_semaphore()
@@ -240,6 +264,8 @@
     def flat(ref):
         return jnp.concatenate([ref[r].astype(jnp.float32) for r in range(requests)], axis=0)
 
+    for copy in early[:4]:
+        copy.wait()
     fields = []
     for ref in (q_ref, k_ref, v_ref, g_ref):
         values = flat(ref).astype(jnp.bfloat16)
@@ -364,6 +390,8 @@
                 at_once // 2, 2, owned, head_dim
             )
 
+    for copy in early[4:]:
+        copy.wait()
     wide_cut = width // chunks
 
     def reduce_scatter(turn, produce):
@@ -594,9 +622,16 @@
             layer_kernel, (wide_size, owned, width, experts, local_experts, held, chunks)
         ),
         out_shape=jax.ShapeDtypeStruct((owned_req, num_steps, width), bf16),
-        in_specs=[hbm] + [vmem] * 10 + [hbm] * 3,
+        in_specs=[hbm] * 5 + [vmem] * 2 + [hbm] * 2 + [vmem] + [hbm] * 4,
         out_specs=vmem,
         scratch_shapes=[
+            pltpu.VMEM(queries.shape, bf16),
+            pltpu.VMEM(keys_in.shape, bf16),
+            pltpu.VMEM(values_in.shape, bf16),
+            pltpu.VMEM(gate_in.shape, bf16),
+            pltpu.VMEM(out_weight.shape, bf16),
+            pltpu.VMEM(residual_in.shape, bf16),
+            pltpu.VMEM(router_weight.shape, bf16),
             pltpu.VMEM((wide_size, owned_req * key_dim, columns), bf16),
             pltpu.VMEM((wide_size, owned, box), bf16),
             pltpu.VMEM((wide_size, owned, box), bf16),
@@ -619,6 +654,7 @@
             pltpu.VMEM((local_experts, slots, hidden_units), bf16),
             pltpu.VMEM((num_z * 2, 2, owned, local_experts * slots), bf16),
             pltpu.VMEM((num_z * 2, 2, owned, local_experts * slots), bf16),
+            pltpu.SemaphoreType.DMA((7,)),
             pltpu.SemaphoreType.DMA,
             pltpu.SemaphoreType.DMA((wide_size - 1,)),
             pltpu.SemaphoreType.DMA((wide_size - 1,)),

time: 77.6 us -> 77.4 us (level)
  no operation moved by 1% of the time
where the time goes in v4:
time: 77.4 us; the launch traced here: 77 us
  Pallas kernels  73.5 us (95%)
  local copies, waits for them, and re-layouts  2.09 us (3%)
  other arithmetic  1.48 us (2%)
    pallas_call x1, Pallas kernels, fused_layer(): pl.pallas_call(functools.partial(layer_kernel, (wide_size, owned, width,...  73.5 us

profile of v4, /device:TPU:0, one launch (start us, length us, event | category | flops | bytes accessed | tf_op | source)
XLA Modules:
  0.0 77.0 jit_solution(8158327203985162247)
XLA Ops:
  0.0 0.7 convert_element_type.5
  0.7 0.8 %pad_maximum_fusion = bf16[4,4,74]{2,1,0:T(4,128)(2,1)S(1)} fusion(bf16[4,4,10]{2,1,0:T(4,128)(2,1)S(1)} %convert_element_type.5, bf16[4,4,32]{2,1,0:T(4,128)(2,1)} %param.23, bf16[4,4,32]{2,1,0:T(4,128)(2,1)} %param.22), kind=kLoop, calls=%fused_computation | loop fusion | flops 7104 | bytes 4736 | tf_op jit(solution)/shard_map/concatenate | solution.py:610
  1.5 0.6 pad.4.facts_ref
  2.1 73.5 %shard_map.154 = bf16[4,4,2048]{2,1,0:T(4,128)(2,1)} custom-call(bf16[16,512,256]{2,1,0:T(8,128)(2,1)} %bitcast.4, bf16[4,4,2048]{2,1,0:T(4,128)(2,1)} %q_hbm.1, bf16[4,4,2048]{2,1,0:T(4,128)(2,1)} %k_hbm.1, bf16[4,4,4096]{2,1,0:T(4,128)(2,1)} %v_hbm.1, bf16[4,4,4096]{2,1,0:T(4,128)(2,1)} %g_hbm.1, bf16[16,128]{1,0:T(8,128)(2,1)} %pad.4.facts_ref, ...), custom_call_target="tpu_custom_call" | custom-call | tf_op jit(solution)/shard_map/pallas_call | solution.py:620
  75.5 1.5 %copy.18 = bf16[4,4,2048]{2,1,0:T(4,128)(2,1)} copy(bf16[4,4,2048]{2,1,0:T(4,128)(2,1)} %shard_map.154) | data formatting | bytes 131072
